TPU v7x, 32 devices: a whole 2x2x4 slice. The times are simulated.
32 devices in a mesh: rows: 8 (over z, x), snap: 4 (over y, core).
Axes of the slice: x: 2, y: 2, z: 4, core: 2. Of those that a mesh axis runs over, the one named last changes fastest.
Arguments:
- snapshots: bfloat16 [12288, 1536], P('rows', 'snap'), may hold values from -6 to 6
- mass: bfloat16 [125, 12288], P(None, 'rows'), may hold values from -0.0048828125 to 0.0048828125
- counts: int32 [8], P('rows'), may hold values from 512 to 1536, as said below
- send_rows: int32 [8, 256], P('rows'), may hold values from 0 to 1535, as said below
- columns: int32 [125, 12288], P(None, 'rows'), may hold values from 0 to 1791, as said below
Outputs:
- gram_band: float32 [3, 1536, 384], P(None, ('snap', 'rows'))
Inputs may be any that keep to these rules, and one draw needn't show every extreme that they name: counts[p] rows of partition p are live; some partition holds 1536 rows. send_rows[p, j] < counts[p]. `columns`: indices from 1536 on address the rows received from the left, then from the right neighbour.
All inputs are finite; a program needn't handle non-finite values.
Results may differ from a plain program's by a relative error of at most 0.003.
Values may be sent and summed in bfloat16 or wider, within the bound.
A program may use at most 64 MiB of HBM per device.

v0:
```python
import jax
import jax.numpy as jnp
from jax import lax
from jax.sharding import PartitionSpec as P

BAND = 3


def extended_2(x, sides, width):
    for axis, dim in sides:
        devices, length = (lax.axis_size(axis), x.shape[dim])
        up = [(i, (i + 1) % devices) for i in range(devices - 1)]
        down = [(j, i) for i, j in up]
        last = lax.slice_in_dim(x, length - width, length, axis=dim)
        initial = lax.slice_in_dim(x, 0, width, axis=dim)
        before = lax.ppermute(last, axis, up)
        after = lax.ppermute(initial, axis, down)
        x = jnp.concatenate([before, x, after], axis=dim)
    return x


def shifted(value, axis, steps):
    count = lax.axis_size(axis)
    pairs = [(source, (source + steps) % count) for source in range(count)]
    return lax.ppermute(value, axis, pairs)


def band_term(masked, visitor):
    return lax.dot_general(
        masked, visitor, (((0,), (0,)), ((), ())), preferred_element_type=jnp.float32
    )


def body(snapshots, mass, counts, send_rows, columns):
    rows_cap = snapshots.shape[0]
    halo_rows = send_rows.shape[1] // 2
    live_rows = lax.broadcasted_iota(jnp.int32, (rows_cap, 1), 0) < counts[0]
    masked = jnp.where(live_rows, snapshots, jnp.zeros_like(snapshots))
    row_index = lax.broadcasted_iota(jnp.int32, columns.shape, 1)
    dense = jnp.zeros((rows_cap, rows_cap + 2 * halo_rows), jnp.float32)
    operator = dense.at[row_index, columns].add(mass.astype(jnp.float32)).astype(jnp.bfloat16)
    outgoing = jnp.take(masked, send_rows[0], axis=0)
    padded = extended_2(outgoing, (("rows", 0),), halo_rows)
    from_left = padded[:halo_rows]
    from_right = padded[3 * halo_rows :]
    extended = jnp.concatenate([masked, from_left, from_right], 0)
    mass_image = jnp.dot(operator, extended, preferred_element_type=jnp.float32)
    mass_image = jnp.where(live_rows, mass_image, jnp.zeros_like(mass_image)).astype(jnp.bfloat16)
    visitor = mass_image
    results = []
    for offset in range(BAND):
        if offset > 0:
            visitor = shifted(visitor, "snap", 1)
        results.append(band_term(masked, visitor))
    stacked = jnp.stack(results)
    stacked = lax.psum_scatter(stacked, "rows", scatter_dimension=1, tiled=True)
    return stacked


def solution(mesh):
    return jax.shard_map(
        body,
        mesh=mesh,
        in_specs=(P("rows", "snap"), P(None, "rows"), P("rows"), P("rows", None), P(None, "rows")),
        out_specs=P(None, ("snap", "rows"), None),
        check_vma=False,
    )
```

profile of v0, /device:TPU:0, one launch (start us, length us, event | category | flops | bytes accessed | tf_op | source)
XLA Modules:
  0.0 1156.3 jit_solution(1594788875770626792)
XLA Ops:
  6.5 0.0 reduce-scatter.2.cloned.1.call-start
  7.2 0.7 compare_select_fusion.1
  7.9 0.7 compare_and_fusion
  8.6 1.5 broadcast_select_fusion
  10.1 0.0 copy-start
  10.1 1.2 gather_fusion
  11.3 0.0 copy-start.3
  11.3 0.1 broadcast_select_fusion.2
  11.5 1.3 collective-permute-start.1
  12.8 5.5 collective-permute-start
  18.2 0.0 copy-done
  18.3 0.1 fusion.8
  18.4 0.0 copy-start.2
  18.4 0.1 iota.14
  18.5 0.0 copy-done.3
  18.5 0.4 and_reduce_fusion
  18.8 0.2 copy-done.2
  19.0 0.2 multiply_reduce_fusion
  19.3 0.0 copy-start.1
  19.3 0.1 broadcast_select_fusion.1
  19.4 0.1 reshape.62
  19.4 0.8 copy-done.1
  20.3 0.4 reshape.64
  20.7 1003.7 %scatter_custom_fusion = f32[2752512]{0:T(1024)} fusion(s32[192000]{0:T(1024)S(1)} %reshape.62, f32[192000]{0:T(1024)S(1)} %reshape.64, f32[]{:T(128)} %constant.9.clone.1), kind=kCustom, calls=%fused_computation.2 | custom fusion | flops 192000 | bytes 11010052
  1024.4 7.2 convert_element_type.12
  1031.6 10.9 reshape.53
  1042.6 0.0 collective-permute-done.1
  1042.6 0.0 collective-permute-done
  1042.6 5.6 fusion.2
  1048.2 0.1 collective-permute-start.2
  1048.2 15.6 %collective-permute-done.2 = bf16[1536,384]{1,0:T(8,128)(2,1)S(1)} collective-permute-done((bf16[1536,384]{1,0:T(8,128)(2,1)S(1)}, bf16[1536,384]{1,0:T(8,128)(2,1)S(1)}, u32[]{:S(2)}, u32[]{:S(2)}) %collective-permute-start.2) | collective-permute-done | bytes 1179680 | tf_op jit(solution)/shard_map/ppermute | solution.py:25
  1063.8 0.0 collective-permute-start.3
  1063.8 0.8 convolution_bitcast_fusion.2
  1064.6 0.8 convolution_bitcast_fusion.1
  1065.4 14.0 %collective-permute-done.3 = bf16[1536,384]{1,0:T(8,128)(2,1)S(1)} collective-permute-done((bf16[1536,384]{1,0:T(8,128)(2,1)S(1)}, bf16[1536,384]{1,0:T(8,128)(2,1)S(1)}, u32[]{:S(2)}, u32[]{:S(2)}) %collective-permute-start.3) | collective-permute-done | bytes 1179680 | tf_op jit(solution)/shard_map/ppermute | solution.py:25
  1079.5 0.8 convolution_bitcast_fusion
  1080.3 1.3 pad_maximum_fusion
  1081.6 0.0 reduce-scatter.2.cloned.1.call-update
  1081.6 67.8 %reduce-scatter.2.cloned.1.call-done = f32[3,48,384]{2,1,0:T(8,128)} async-done(((f32[3,384,384]{2,1,0:T(8,128)}), f32[3,48,384]{2,1,0:T(8,128)}) %reduce-scatter.2.cloned.1.call-update) | async-done | bytes 221200 | tf_op jit(solution)/shard_map/reduce_scatter | solution.py:56
  (3 shorter events, 0.0 us)
Async XLA Ops:
  6.5 1142.9 %reduce-scatter.2.cloned.1.call-start = ((), (), s32[]{:S(2)}) async-start(), calls=%async_computation.1 | async-start | bytes 1990656 | tf_op jit(solution)/shard_map/reduce_scatter | solution.py:56
  10.1 8.1 copy-start
  11.3 7.1 copy-start.3
  11.5 1031.1 %collective-permute-start.1 = (bf16[128,384]{1,0:T(8,128)(2,1)S(1)}, bf16[128,384]{1,0:T(8,128)(2,1)S(1)}, u32[]{:S(2)}, u32[]{:S(2)}) collective-permute-start(bf16[128,384]{1,0:T(8,128)(2,1)S(1)} %get-tuple-element.6), channel_id=1, source_target_pairs={{4,0},{8,4},{12,8},{16,12},{20,16},{24,20},{28,24},{5,1},{9,5},{13... | collective-permute-start | bytes 294920 | tf_op jit(solution)/shard_map/ppermute | solution.py:17
  12.8 1029.8 %collective-permute-start = (bf16[128,384]{1,0:T(8,128)(2,1)S(1)}, bf16[128,384]{1,0:T(8,128)(2,1)S(1)}, u32[]{:S(2)}, u32[]{:S(2)}) collective-permute-start(bf16[128,384]{1,0:T(8,128)(2,1)S(1)} %get-tuple-element.5), channel_id=1, source_target_pairs={{0,4},{4,8},{8,12},{12,16},{16,20},{20,24},{24,28},{1,5},{5,9},{9,... | collective-permute-start | bytes 294920 | tf_op jit(solution)/shard_map/ppermute | solution.py:16
  18.4 0.7 copy-start.2
  19.3 1.0 copy-start.1
  1048.2 15.7 %collective-permute-start.2 = (bf16[1536,384]{1,0:T(8,128)(2,1)S(1)}, bf16[1536,384]{1,0:T(8,128)(2,1)S(1)}, u32[]{:S(2)}, u32[]{:S(2)}) collective-permute-start(bf16[1536,384]{1,0:T(8,128)(2,1)S(1)} %fusion.2), channel_id=1, source_target_pairs={{0,1},{1,2},{2,3},{3,0},{4,5},{5,6},{6,7},{7,4},{8,9},{9,10},{10,1... | collective-permute-start | bytes 3538952 | tf_op jit(solution)/shard_map/ppermute | solution.py:25
  1063.8 15.6 %collective-permute-start.3 = (bf16[1536,384]{1,0:T(8,128)(2,1)S(1)}, bf16[1536,384]{1,0:T(8,128)(2,1)S(1)}, u32[]{:S(2)}, u32[]{:S(2)}) collective-permute-start(bf16[1536,384]{1,0:T(8,128)(2,1)S(1)} %collective-permute-done.2), channel_id=1, source_target_pairs={{0,1},{1,2},{2,3},{3,0},{4,5},{5,6},{6,7},{7,4},{8,9},{9,10},{10,1... | collective-permute-start | bytes 3538952 | tf_op jit(solution)/shard_map/ppermute | solution.py:25
Sparse Core Ops, SparseCore 0:
  1081.7 67.6 reduce-scatter.1
where the time goes:
time: 1160 us
  other arithmetic  1020 us (88%)
  waiting for transfers between devices  97.5 us (8%)
  between operations  14.2 us (1%)
  local copies, waits for them, and re-layouts  13.7 us (1%)
    unnamed x4, other arithmetic  1000 us
    reduce_scatter x1, waiting for transfers between devices, body(): stacked = lax.psum_scatter(stacked, 'rows', scatter_dimension=1, tiled=True)  67.8 us
    ppermute x2, waiting for transfers between devices, shifted(): return lax.ppermute(value, axis, pairs)  29.6 us
  transfers between devices with their start and end apart: 5, of which 3 were waited for; matrix products, arithmetic and copies ran while one was open for 89% of the time, Pallas kernels for 0%

commit v1 on v0

v1 whole, which is shorter than its diff:
```python
import functools

import jax
import jax.numpy as jnp
from jax import lax
from jax.experimental import pallas as pl
from jax.experimental.pallas import tpu as pltpu
from jax.sharding import PartitionSpec as P

BAND = 3
LANES = 128
MESH = pl.DeviceIdType.MESH


def operator_kernel(cols_ref, mass_ref, op_ref, cols_pad, mass_pad, cols_t, mass_t, acc):
    nnz, tile = cols_ref.shape
    tiles = op_ref.shape[1] // LANES
    cols_pad[...] = jnp.zeros_like(cols_pad)
    mass_pad[...] = jnp.zeros_like(mass_pad)
    cols_pad[:nnz, :] = cols_ref[...]
    mass_pad[:nnz, :] = mass_ref[...].astype(jnp.float32)
    cols_t[...] = cols_pad[...].T
    mass_t[...] = mass_pad[...].T
    step = 16
    iota = lax.broadcasted_iota(jnp.int32, (LANES, LANES), 0).astype(jnp.float32).astype(jnp.bfloat16)
    iota_hi = iota[:16]
    zero = jnp.zeros((16, LANES), jnp.bfloat16)
    one = jnp.ones((LANES, LANES), jnp.bfloat16)
    zeros = jnp.zeros((LANES, LANES), jnp.bfloat16)

    def group(g, carry):
        base = pl.multiple_of(g * step, step)
        c = cols_t[pl.ds(base, step), :]
        low = (c & (LANES - 1)).astype(jnp.float32)
        high = (c // LANES).astype(jnp.float32)
        m = mass_t[pl.ds(base, step), :]
        for i in range(step):
            low_b = jnp.broadcast_to(low[i : i + 1], (16, LANES)).astype(jnp.bfloat16)
            high_b = jnp.broadcast_to(high[i : i + 1], (16, LANES)).astype(jnp.bfloat16)
            m_b = jnp.broadcast_to(m[i : i + 1], (16, LANES)).astype(jnp.bfloat16)
            left = jnp.where(high_b == iota_hi, m_b, zero)
            right = jnp.where(jnp.concatenate([low_b] * (LANES // 16), 0) == iota, one, zeros)
            out = lax.dot_general(left, right, (((1,), (1,)), ((), ())), preferred_element_type=jnp.float32)
            acc[pl.ds(pl.multiple_of(base * 16 + i * 16, 16), 16), :] = out
        return carry

    lax.fori_loop(0, tile // step, group, 0)
    for h in range(tiles):
        op_ref[:, h * LANES : (h + 1) * LANES] = acc[pl.ds(h, tile, stride=16), :].astype(op_ref.dtype)


def build_operator(columns, mass, width):
    nnz, rows_cap = columns.shape
    tile = LANES
    return pl.pallas_call(
        operator_kernel,
        grid=(rows_cap // tile,),
        out_shape=jax.ShapeDtypeStruct((rows_cap, width), jnp.bfloat16),
        in_specs=[pl.BlockSpec((nnz, tile), lambda i: (0, i))] * 2,
        out_specs=pl.BlockSpec((tile, width), lambda i: (i, 0)),
        scratch_shapes=[
            pltpu.VMEM((LANES, tile), jnp.int32),
            pltpu.VMEM((LANES, tile), jnp.float32),
            pltpu.VMEM((tile, LANES), jnp.int32),
            pltpu.VMEM((tile, LANES), jnp.float32),
            pltpu.VMEM((tile * 16, LANES), jnp.float32),
        ],
        compiler_params=pltpu.CompilerParams(vmem_limit_bytes=16 * 1024 * 1024),
        cost_estimate=pl.CostEstimate(flops=60_000_000_000, bytes_accessed=7_000_000, transcendentals=0),
    )(columns, mass)


def sum_kernel(parts, snaps, part_ref, out_ref, recv, stage, send_sem, recv_sem, shift_send, shift_recv):
    me = lax.axis_index("rows")
    here = lax.axis_index("snap")
    share = out_ref.shape[1]
    barrier = pltpu.get_barrier_semaphore()

    def greet(d, carry):
        pl.semaphore_signal(barrier, inc=1, device_id=(lax.rem(me + d, parts), here), device_id_type=MESH)
        return carry

    lax.fori_loop(1, parts, greet, 0)
    for k in range(1, BAND):
        pl.semaphore_signal(barrier, inc=1, device_id=(me, lax.rem(here + snaps - k, snaps)), device_id_type=MESH)
    pl.semaphore_wait(barrier, parts - 1 + BAND - 1)

    def copy(d):
        to = lax.rem(me + d, parts)
        return pltpu.make_async_remote_copy(
            src_ref=part_ref.at[to],
            dst_ref=recv.at[d],
            send_sem=send_sem.at[d],
            recv_sem=recv_sem.at[d],
            device_id=(to, here),
            device_id_type=MESH,
        )

    def start(d, carry):
        copy(d).start()
        return carry

    lax.fori_loop(1, parts, start, 0)

    def add(d, total):
        copy(d).wait_recv()
        return total + recv[d].astype(jnp.float32)

    stage[...] = lax.fori_loop(1, parts, add, part_ref[me].astype(jnp.float32))
    shifts = []
    for k in range(1, BAND):
        shift = pltpu.make_async_remote_copy(
            src_ref=stage.at[k],
            dst_ref=out_ref.at[k],
            send_sem=shift_send.at[k],
            recv_sem=shift_recv.at[k],
            device_id=(me, lax.rem(here + k, snaps)),
            device_id_type=MESH,
        )
        shift.start()
        shifts.append(shift)
    out_ref[0] = stage[0]

    def sent(d, carry):
        copy(d).wait_send()
        return carry

    lax.fori_loop(1, parts, sent, 0)
    for shift in shifts:
        shift.wait()


def sum_terms(terms, parts, snaps):
    share, width = terms.shape[2:]
    return pl.pallas_call(
        functools.partial(sum_kernel, parts, snaps),
        out_shape=jax.ShapeDtypeStruct((BAND, share, width), jnp.float32),
        in_specs=[pl.BlockSpec(memory_space=pltpu.VMEM)],
        out_specs=pl.BlockSpec(memory_space=pltpu.VMEM),
        scratch_shapes=[
            pltpu.VMEM(terms.shape, terms.dtype),
            pltpu.VMEM((BAND, share, width), jnp.float32),
            pltpu.SemaphoreType.DMA((parts,)),
            pltpu.SemaphoreType.DMA((parts,)),
            pltpu.SemaphoreType.DMA((BAND,)),
            pltpu.SemaphoreType.DMA((BAND,)),
        ],
        compiler_params=pltpu.CompilerParams(
            collective_id=0, has_side_effects=True, vmem_limit_bytes=24 * 1024 * 1024
        ),
    )(terms)


def shifted(value, axis, steps):
    count = lax.axis_size(axis)
    pairs = [(source, (source + steps) % count) for source in range(count)]
    return lax.ppermute(value, axis, pairs)


def band_term(masked, image):
    return lax.dot_general(masked, image, (((0,), (0,)), ((), ())), preferred_element_type=jnp.float32)


def body(snapshots, mass, counts, send_rows, columns):
    parts, snaps = lax.axis_size("rows"), lax.axis_size("snap")
    rows_cap, width = snapshots.shape
    halo_rows = send_rows.shape[1] // 2
    live_rows = lax.broadcasted_iota(jnp.int32, (rows_cap, 1), 0) < counts[0]
    masked = jnp.where(live_rows, snapshots, jnp.zeros_like(snapshots))
    outgoing = jnp.take(masked, send_rows[0], axis=0)
    up = [(i, i + 1) for i in range(parts - 1)]
    down = [(j, i) for i, j in up]
    from_left = lax.ppermute(outgoing[halo_rows:], "rows", up)
    from_right = lax.ppermute(outgoing[:halo_rows], "rows", down)
    lefts = [masked]
    for k in range(1, BAND):
        lefts.append(shifted(lefts[-1], "snap", -1))
    operator = build_operator(columns, mass, rows_cap + 2 * halo_rows)
    extended = jnp.concatenate([masked, from_left, from_right], 0)
    image = jnp.dot(operator, extended, preferred_element_type=jnp.float32)
    image = jnp.where(live_rows, image, jnp.zeros_like(image)).astype(jnp.bfloat16)
    terms = jnp.stack([band_term(left, image).reshape(parts, width // parts, width) for left in lefts], 1)
    return sum_terms(terms.astype(jnp.bfloat16), parts, snaps)


def solution(mesh):
    return jax.shard_map(
        body,
        mesh=mesh,
        in_specs=(P("rows", "snap"), P(None, "rows"), P("rows"), P("rows", None), P(None, "rows")),
        out_specs=P(None, ("snap", "rows"), None),
        check_vma=False,
    )
```

time: 1160 us -> 98.4 us (0.08)
  the two profiles are of different devices: /device:TPU:0 before, /device:TPU:15 now
where the time goes in v1:
time: 98.4 us; the launch traced here: 98.2 us
  Pallas kernels  71 us (72%)
  waiting for transfers between devices  9.33 us (9%)
  matrix products  6.68 us (7%)
  starting transfers between devices  6.66 us (7%)
  local copies, waits for them, and re-layouts  1.9 us (2%)
  other arithmetic  1.8 us (2%)
    pallas_call x1, Pallas kernels, build_operator(): pl.pallas_call(operator_kernel, grid=(rows_cap // tile,), out_shape=jax.S...  43.2 us
    pallas_call x1, Pallas kernels, sum_terms(): pl.pallas_call(functools.partial(sum_kernel, parts, snaps), out_shape=jax...  27.8 us
    ppermute x2, waiting for transfers between devices, shifted(): return lax.ppermute(value, axis, pairs)  9.33 us
    dot_general x3, matrix products, band_term(): lax.dot_general(masked, image, (((0,), (0,)), ((), ())), preferred_elemen...  3.65 us
    ppermute x1, starting transfers between devices, body(): from_left = lax.ppermute(outgoing[halo_rows:], 'rows', up)  3.18 us
    dot_general x1, matrix products, body(): image = jnp.dot(operator, extended, preferred_element_type=jnp.float32)  3.03 us
    ppermute x1, starting transfers between devices, body(): from_right = lax.ppermute(outgoing[:halo_rows], 'rows', down)  2.11 us
  transfers between devices with their start and end apart: 4, of which 1 were waited for; matrix products, arithmetic and copies ran while one was open for 7% of the time, Pallas kernels for 44%

profile of v1, /device:TPU:15, one launch (start us, length us, event | category | flops | bytes accessed | tf_op | source)
XLA Modules:
  0.0 98.2 jit_solution(8145183186618667485)
XLA Ops:
  0.7 0.0 copy-start.2
  0.7 1.6 %broadcast_select_fusion = bf16[1536,384]{1,0:T(8,128)(2,1)S(1)} fusion(bf16[1536,384]{1,0:T(8,128)(2,1)} %param.5, pred[1536]{0:T(1024)(128)(4,1)S(1)} %iota_compare_fusion), kind=kLoop, calls=%fused_computation.11 | loop fusion | flops 589824 | bytes 2360832 | tf_op jit(solution)/shard_map/jit(_where)/select_n | solution.py:169
  2.2 0.7 collective-permute-start.2
  3.0 0.0 copy-done.2
  3.0 0.0 copy-start
  3.0 0.0 copy-start.1
  3.0 1.2 %gather_fusion = bf16[256,384]{1,0:T(8,128)(2,1)S(1)} fusion(bf16[1536,384]{1,0:T(8,128)(2,1)S(1)} %broadcast_select_fusion, s32[1024]{0:T(1024)S(1)} %pad_clamp_fusion), kind=kCustom, calls=%fused_computation | custom fusion | bytes 394240 | tf_op jit(solution)/shard_map/jit(_take)/gather | solution.py:170
  4.2 0.1 broadcast_select_fusion.1
  4.3 3.2 %collective-permute-start = (bf16[128,384]{1,0:T(8,128)(2,1)S(1)}, bf16[128,384]{1,0:T(8,128)(2,1)S(1)}, u32[]{:S(2)}, u32[]{:S(2)}) collective-permute-start(bf16[128,384]{1,0:T(8,128)(2,1)S(1)} %get-tuple-element.5), channel_id=1, source_target_pairs={{0,4},{4,8},{8,12},{12,16},{16,20},{20,24},{24,28},{1,5},{5,9},{9,... | collective-permute-start | bytes 294920 | tf_op jit(solution)/shard_map/ppermute | solution.py:173
  7.5 2.1 %collective-permute-start.1 = (bf16[128,384]{1,0:T(8,128)(2,1)S(1)}, bf16[128,384]{1,0:T(8,128)(2,1)S(1)}, u32[]{:S(2)}, u32[]{:S(2)}) collective-permute-start(bf16[128,384]{1,0:T(8,128)(2,1)S(1)} %get-tuple-element.6), channel_id=1, source_target_pairs={{4,0},{8,4},{12,8},{16,12},{20,16},{24,20},{28,24},{5,1},{9,5},{13... | collective-permute-start | bytes 294920 | tf_op jit(solution)/shard_map/ppermute | solution.py:174
  9.6 0.0 copy-done
  9.6 0.0 copy-done.1
  9.6 43.2 %shard_map.55 = bf16[1536,1792]{1,0:T(8,128)(2,1)S(1)} custom-call(s32[125,1536]{1,0:T(8,128)S(1)} %copy-done, bf16[125,1536]{1,0:T(8,128)(2,1)S(1)} %copy-done.1), custom_call_target="tpu_custom_call" | custom-call | flops 60000002048 | bytes 7000000 | tf_op jit(solution)/shard_map/pallas_call | solution.py:55
  52.9 0.0 collective-permute-done.2
  52.9 0.6 collective-permute-start.3
  53.5 0.0 collective-permute-done
  53.5 0.0 collective-permute-done.1
  53.5 3.0 %fusion = bf16[1536,384]{1,0:T(8,128)(2,1)S(1)} fusion(bf16[1536,1792]{1,0:T(8,128)(2,1)S(1)} %shard_map.55, bf16[128,384]{1,0:T(8,128)(2,1)S(1)} %collective-permute-done.1, bf16[128,384]{1,0:T(8,128)(2,1)S(1)} %collective-permute-done, bf16[1536,384]{1,0:T(8,128)(2,1)S(1)} %broadcast_select_fusion, pred[1536]{0:T(1024)(128)(4,1)S(1)} %iota_compare_fusion), kind=kOutput, calls=%fused_computation.2 | convolution fusion | flops 2119237632 | bytes 8062464 | tf_op jit(solution)/shard_map/dot_general | solution.py:180
  56.6 0.8 convolution_convert_fusion.2
  57.4 2.1 %convolution_convert_fusion.1 = bf16[384,384]{1,0:T(8,128)(2,1)S(1)} fusion(bf16[1536,384]{1,0:T(8,128)(2,1)} %collective-permute-done.2, bf16[1536,384]{1,0:T(8,128)(2,1)S(1)} %fusion), kind=kOutput, calls=%fused_computation.9 | convolution fusion | flops 453132288 | bytes 2654208 | tf_op jit(solution)/shard_map/dot_general | solution.py:161
  59.5 9.3 %collective-permute-done.3 = bf16[1536,384]{1,0:T(8,128)(2,1)S(1)} collective-permute-done((bf16[1536,384]{1,0:T(8,128)(2,1)}, bf16[1536,384]{1,0:T(8,128)(2,1)S(1)}, u32[]{:S(2)}, u32[]{:S(2)}) %collective-permute-start.3) | collective-permute-done | bytes 1179680 | tf_op jit(solution)/shard_map/ppermute | solution.py:157
  68.8 0.8 convolution_convert_fusion
  69.6 0.1 pad_maximum_fusion.part_ref
  69.7 27.8 %shard_map.56 = f32[3,48,384]{2,1,0:T(8,128)S(1)} custom-call(bf16[8,3,48,384]{3,2,1,0:T(8,128)(2,1)S(1)} %pad_maximum_fusion.part_ref), custom_call_target="tpu_custom_call" | custom-call | tf_op jit(solution)/shard_map/pallas_call | solution.py:135
  97.5 0.7 copy.8
  (5 shorter events, 0.0 us)
Async XLA Ops:
  0.7 2.3 %copy-start.2 = (s32[1,256]{1,0:T(1,128)S(1)}, s32[1,256]{1,0:T(1,128)}, u32[]{:S(2)}) copy-start(s32[1,256]{1,0:T(1,128)} %param.8) | copy-start | bytes 3076
  2.2 50.6 %collective-permute-start.2 = (bf16[1536,384]{1,0:T(8,128)(2,1)S(1)}, bf16[1536,384]{1,0:T(8,128)(2,1)}, u32[]{:S(2)}, u32[]{:S(2)}) collective-permute-start(bf16[1536,384]{1,0:T(8,128)(2,1)S(1)} %broadcast_select_fusion), channel_id=1, source_target_pairs={{0,3},{1,0},{2,1},{3,2},{4,7},{5,4},{6,5},{7,6},{8,11},{9,8},{10,9... | collective-permute-start | bytes 3538952 | tf_op jit(solution)/shard_map/ppermute | solution.py:157
  3.0 6.6 %copy-start = (s32[125,1536]{1,0:T(8,128)S(1)}, s32[125,1536]{1,0:T(8,128)}, u32[]{:S(2)}) copy-start(s32[125,1536]{1,0:T(8,128)} %cols_ref.1) | copy-start | bytes 2304004
  3.0 6.6 %copy-start.1 = (bf16[125,1536]{1,0:T(8,128)(2,1)S(1)}, bf16[125,1536]{1,0:T(8,128)(2,1)}, u32[]{:S(2)}) copy-start(bf16[125,1536]{1,0:T(8,128)(2,1)} %mass_ref.1) | copy-start | bytes 1152004
  4.3 49.2 %collective-permute-start = (bf16[128,384]{1,0:T(8,128)(2,1)S(1)}, bf16[128,384]{1,0:T(8,128)(2,1)S(1)}, u32[]{:S(2)}, u32[]{:S(2)}) collective-permute-start(bf16[128,384]{1,0:T(8,128)(2,1)S(1)} %get-tuple-element.5), channel_id=1, source_target_pairs={{0,4},{4,8},{8,12},{12,16},{16,20},{20,24},{24,28},{1,5},{5,9},{9,... | collective-permute-start | bytes 294920 | tf_op jit(solution)/shard_map/ppermute | solution.py:173
  7.5 46.0 %collective-permute-start.1 = (bf16[128,384]{1,0:T(8,128)(2,1)S(1)}, bf16[128,384]{1,0:T(8,128)(2,1)S(1)}, u32[]{:S(2)}, u32[]{:S(2)}) collective-permute-start(bf16[128,384]{1,0:T(8,128)(2,1)S(1)} %get-tuple-element.6), channel_id=1, source_target_pairs={{4,0},{8,4},{12,8},{16,12},{20,16},{24,20},{28,24},{5,1},{9,5},{13... | collective-permute-start | bytes 294920 | tf_op jit(solution)/shard_map/ppermute | solution.py:174
  52.9 15.9 %collective-permute-start.3 = (bf16[1536,384]{1,0:T(8,128)(2,1)}, bf16[1536,384]{1,0:T(8,128)(2,1)S(1)}, u32[]{:S(2)}, u32[]{:S(2)}) collective-permute-start(bf16[1536,384]{1,0:T(8,128)(2,1)} %collective-permute-done.2), channel_id=1, source_target_pairs={{0,3},{1,0},{2,1},{3,2},{4,7},{5,4},{6,5},{7,6},{8,11},{9,8},{10,9... | collective-permute-start | bytes 3538952 | tf_op jit(solution)/shard_map/ppermute | solution.py:157

commit v2 on v0

v2 whole, which is shorter than its diff:
```python
import functools

import jax
import jax.numpy as jnp
from jax import lax
from jax.experimental import pallas as pl
from jax.experimental.pallas import tpu as pltpu
from jax.sharding import PartitionSpec as P

BAND = 3
LANES = 128
STEP = 16
MESH = pl.DeviceIdType.MESH
NT = (((1,), (1,)), ((), ()))
TN = (((0,), (0,)), ((), ()))


def operator_chunk(cols_ref, mass_ref, op_ref, start, cols_pad, mass_pad, cols_t, mass_t, acc):
    nnz = cols_ref.shape[0]
    tile = cols_t.shape[0]
    tiles = op_ref.shape[1] // LANES
    cols_pad[:nnz, :] = cols_ref[:, pl.ds(start, tile)]
    mass_pad[:nnz, :] = mass_ref[:, pl.ds(start, tile)].astype(jnp.float32)
    cols_t[...] = cols_pad[...].T
    mass_t[...] = mass_pad[...].T
    iota = lax.broadcasted_iota(jnp.int32, (LANES, LANES), 0).astype(jnp.float32).astype(jnp.bfloat16)
    zero = jnp.zeros((STEP, LANES), jnp.bfloat16)
    one = jnp.ones((LANES, LANES), jnp.bfloat16)
    zeros = jnp.zeros((LANES, LANES), jnp.bfloat16)

    def group(g, carry):
        base = pl.multiple_of(g * STEP, STEP)
        c = cols_t[pl.ds(base, STEP), :]
        low = (c & (LANES - 1)).astype(jnp.float32)
        high = (c >> 7).astype(jnp.float32)
        m = mass_t[pl.ds(base, STEP), :]

        def wide(x, i):
            return jnp.broadcast_to(x[i : i + 1], (16, LANES)).astype(jnp.bfloat16)

        def left(i):
            return jnp.where(wide(high, i) == iota[:16], wide(m, i), zero)

        def right(i):
            return jnp.where(jnp.concatenate([wide(low, i)] * (LANES // 16), 0) == iota, one, zeros)

        for i in range(0, STEP, 2):
            out = lax.dot_general(
                jnp.concatenate([left(i), left(i + 1)], 0),
                jnp.concatenate([right(i), right(i + 1)], 0),
                NT,
                preferred_element_type=jnp.float32,
            )
            at = pl.multiple_of(base * 16 + i * 16, 32)
            acc[pl.ds(at, 16), :] = out[:16, :LANES]
            acc[pl.ds(at + 16, 16), :] = out[16:, LANES:]
        return carry

    lax.fori_loop(0, tile // STEP, group, 0)
    for h in range(tiles):
        op_ref[pl.ds(start, tile), h * LANES : (h + 1) * LANES] = acc[pl.ds(h, tile, stride=16), :].astype(op_ref.dtype)


def kernel(
    parts, snaps, snap_ref, out_rows_ref, cols_ref, mass_ref, counts_ref, out_ref,
    ext, op, x1, x2, image, gram, terms, recv, stage,
    cols_pad, mass_pad, cols_t, mass_t, acc,
    halo_send, halo_recv, x_send, x_recv, op_send, op_recv, term_send, term_recv, shift_send, shift_recv,
):
    me = lax.axis_index("rows")
    here = lax.axis_index("snap")
    rows_cap, width = snap_ref.shape
    halo = out_rows_ref.shape[0] // 2
    share = out_ref.shape[1]
    half = rows_cap // 2
    tile = LANES
    chunks = half // tile
    count = counts_ref[0]
    odd = lax.rem(here, 2)
    mate = here + 1 - 2 * odd

    def remote(src, dst, send, arrive, row, snap):
        return pltpu.make_async_remote_copy(
            src_ref=src, dst_ref=dst, send_sem=send, recv_sem=arrive, device_id=(row, snap), device_id_type=MESH
        )

    barrier = pltpu.get_barrier_semaphore()

    def greet(d, carry):
        pl.semaphore_signal(barrier, inc=1, device_id=(lax.rem(me + d, parts), here), device_id_type=MESH)
        return carry

    lax.fori_loop(1, parts, greet, 0)
    offsets = sorted({k % snaps for k in (1, 2, -1, -2)})
    for k in offsets:
        pl.semaphore_signal(barrier, inc=1, device_id=(me, lax.rem(here + k, snaps)), device_id_type=MESH)
    pl.semaphore_wait(barrier, parts - 1 + len(offsets))

    def back(k):
        return lax.rem(here + snaps - k, snaps)

    first = remote(snap_ref, x1, x_send.at[0], x_recv.at[0], me, back(1))
    second = remote(snap_ref, x2, x_send.at[1], x_recv.at[1], me, back(2))
    relay = remote(x1, x2, x_send.at[2], x_recv.at[1], me, back(1))
    up = remote(
        out_rows_ref.at[pl.ds(halo, halo)], ext.at[pl.ds(rows_cap, halo)],
        halo_send.at[0], halo_recv.at[0], lax.rem(me + 1, parts), here,
    )
    down = remote(
        out_rows_ref.at[pl.ds(0, halo)], ext.at[pl.ds(rows_cap + halo, halo)],
        halo_send.at[1], halo_recv.at[1], lax.rem(me + parts - 1, parts), here,
    )
    up.start()
    down.start()
    first.start()

    @pl.when(odd == 1)
    def _():
        second.start()

    cols_pad[...] = jnp.zeros_like(cols_pad)
    mass_pad[...] = jnp.zeros_like(mass_pad)
    row = lax.broadcasted_iota(jnp.int32, (tile, width), 0)

    def mask(t, carry):
        at = pl.multiple_of(t * tile, tile)
        ext[pl.ds(at, tile), :] = jnp.where(row + at < count, snap_ref[pl.ds(at, tile), :].astype(jnp.float32), 0.0).astype(ext.dtype)
        return carry

    lax.fori_loop(0, rows_cap // tile, mask, 0)

    def lend(t):
        at = pl.multiple_of(odd * half + t * tile, tile)
        rows = op.at[pl.ds(at, tile)]
        return remote(rows, rows, op_send.at[t], op_recv.at[t], me, mate)

    def build(t, carry):
        at = pl.multiple_of(odd * half + t * tile, tile)
        operator_chunk(cols_ref, mass_ref, op, at, cols_pad, mass_pad, cols_t, mass_t, acc)
        lend(t).start()
        return carry

    lax.fori_loop(0, chunks, build, 0)

    up.wait()
    down.wait()

    @pl.when(me == 0)
    def _():
        ext[pl.ds(rows_cap, halo), :] = jnp.zeros((halo, width), ext.dtype)

    @pl.when(me == parts - 1)
    def _():
        ext[pl.ds(rows_cap + halo, halo), :] = jnp.zeros((halo, width), ext.dtype)

    big = 2 * tile
    row_big = lax.broadcasted_iota(jnp.int32, (big, width), 0)

    def multiply(at):
        value = jnp.dot(op[pl.ds(at, big), :], ext[...], preferred_element_type=jnp.float32)
        image[pl.ds(at, big), :] = jnp.where(row_big + at < count, value, 0.0).astype(image.dtype)

    def own(t, carry):
        multiply(pl.multiple_of(odd * half + t * big, big))
        return carry

    def lent(t, carry):
        lend(2 * t).wait_recv()
        lend(2 * t + 1).wait_recv()
        multiply(pl.multiple_of((1 - odd) * half + t * big, big))
        return carry

    lax.fori_loop(0, half // big, own, 0)
    lax.fori_loop(0, half // big, lent, 0)

    def term(k, d):
        to = lax.rem(me + d, parts)
        return remote(terms.at[k, to], recv.at[k, d], term_send.at[k, d], term_recv.at[k, d], to, here)

    def band(k, x_ref):
        gram[...] = lax.dot_general(x_ref[...], image[...], TN, preferred_element_type=jnp.float32)
        for q in range(parts):
            terms[k, q] = gram[q * share : (q + 1) * share, :].astype(terms.dtype)

        def start(d, carry):
            term(k, d).start()
            return carry

        lax.fori_loop(1, parts, start, 0)

    band(0, snap_ref)
    first.wait()

    @pl.when(odd == 1)
    def _():
        relay.start()

    band(1, x1)
    second.wait_recv()
    band(2, x2)

    def shift(k):
        return remote(stage.at[k], out_ref.at[k], shift_send.at[k], shift_recv.at[k], me, lax.rem(here + k, snaps))

    for k in range(BAND):

        def add(d, total):
            term(k, d).wait_recv()
            return total + recv[k, d].astype(jnp.float32)

        total = lax.fori_loop(1, parts, add, terms[k, me].astype(jnp.float32))
        if k == 0:
            out_ref[0] = total
        else:
            stage[k] = total
            shift(k).start()

    @pl.when(odd == 1)
    def _():
        second.wait_send()
        relay.wait_send()

    def lent_sent(t, carry):
        lend(t).wait_send()
        return carry

    lax.fori_loop(0, chunks, lent_sent, 0)

    def sent(d, carry):
        for k in range(BAND):
            term(k, d).wait_send()
        return carry

    lax.fori_loop(1, parts, sent, 0)
    for k in range(1, BAND):
        shift(k).wait()


def body(snapshots, mass, counts, send_rows, columns):
    parts, snaps = lax.axis_size("rows"), lax.axis_size("snap")
    rows_cap, width = snapshots.shape
    halo2 = send_rows.shape[1]
    share = width // parts
    wide = rows_cap + halo2
    chunks = rows_cap // 2 // LANES
    outgoing = jnp.take(snapshots, send_rows[0], axis=0)
    bf16, f32 = jnp.bfloat16, jnp.float32
    vmem = pl.BlockSpec(memory_space=pltpu.VMEM)
    return pl.pallas_call(
        functools.partial(kernel, parts, snaps),
        out_shape=jax.ShapeDtypeStruct((BAND, share, width), f32),
        in_specs=[vmem] * 4 + [pl.BlockSpec(memory_space=pltpu.SMEM)],
        out_specs=vmem,
        scratch_shapes=[
            pltpu.VMEM((wide, width), bf16),
            pltpu.VMEM((rows_cap, wide), bf16),
            pltpu.VMEM((rows_cap, width), bf16),
            pltpu.VMEM((rows_cap, width), bf16),
            pltpu.VMEM((rows_cap, width), bf16),
            pltpu.VMEM((width, width), f32),
            pltpu.VMEM((BAND, parts, share, width), bf16),
            pltpu.VMEM((BAND, parts, share, width), bf16),
            pltpu.VMEM((BAND, share, width), f32),
            pltpu.VMEM((LANES, LANES), jnp.int32),
            pltpu.VMEM((LANES, LANES), f32),
            pltpu.VMEM((LANES, LANES), jnp.int32),
            pltpu.VMEM((LANES, LANES), f32),
            pltpu.VMEM((LANES * 16, LANES), f32),
            pltpu.SemaphoreType.DMA((2,)),
            pltpu.SemaphoreType.DMA((2,)),
            pltpu.SemaphoreType.DMA((3,)),
            pltpu.SemaphoreType.DMA((2,)),
            pltpu.SemaphoreType.DMA((chunks,)),
            pltpu.SemaphoreType.DMA((chunks,)),
            pltpu.SemaphoreType.DMA((BAND, parts)),
            pltpu.SemaphoreType.DMA((BAND, parts)),
            pltpu.SemaphoreType.DMA((BAND,)),
            pltpu.SemaphoreType.DMA((BAND,)),
        ],
        compiler_params=pltpu.CompilerParams(
            collective_id=0, has_side_effects=True, vmem_limit_bytes=48 * 1024 * 1024
        ),
    )(snapshots, outgoing, columns, mass, counts)


def solution(mesh):
    return jax.shard_map(
        body,
        mesh=mesh,
        in_specs=(P("rows", "snap"), P(None, "rows"), P("rows"), P("rows", None), P(None, "rows")),
        out_specs=P(None, ("snap", "rows"), None),
        check_vma=False,
    )
```

time: 1160 us -> 56.6 us (0.05)
  other arithmetic: 1020 us -> 1.48 us
  waiting for transfers between devices: 97.5 us -> 0 us
  Pallas kernels: 0 us -> 49.8 us
  between operations: 14.2 us -> 0.84 us
    unnamed x4 -> x0, other arithmetic: 1000 us -> none
    reduce_scatter x1 -> x0, waiting for transfers between devices: 67.8 us -> none  [body(): stacked = lax.psum_scatter(stacked, 'rows', scatter_dimension=1, tiled=True)]
    pallas_call x0 -> x1, Pallas kernels: none -> 49.8 us  [body(): pl.pallas_call(functools.partial(kernel, parts, snaps), out_shape=jax.Sha...]
    ppermute x4 -> x0, waiting for transfers between devices: 29.7 us -> none  [the longest x2 29.6 us: shifted(): return lax.ppermute(value, axis, pairs)]
  transfers between devices with their start and end apart: 5 -> 0, of which waited for: 3 -> 0; matrix products, arithmetic and copies ran while one was open for 89% -> 0% of each run, Pallas kernels for 0% -> 0%
where the time goes in v2:
time: 56.6 us; the launch traced here: 56.4 us
  Pallas kernels  49.8 us (88%)
  local copies, waits for them, and re-layouts  4.25 us (8%)
  other arithmetic  1.48 us (3%)
  between operations  0.84 us (1%)
    pallas_call x1, Pallas kernels, body(): pl.pallas_call(functools.partial(kernel, parts, snaps), out_shape=jax.Sha...  49.8 us
    gather x1, local copies, waits for them, and re-layouts, body(): outgoing = jnp.take(snapshots, send_rows[0], axis=0)  2.57 us
    unnamed x7, local copies, waits for them, and re-layouts  1.69 us

profile of v2, /device:TPU:0, one launch (start us, length us, event | category | flops | bytes accessed | tf_op | source)
XLA Modules:
  0.0 56.4 jit_solution(13626623355915478594)
XLA Ops:
  0.0 0.0 copy-start
  0.0 0.0 copy-start.1
  0.8 0.7 %compare_and_fusion = pred[256]{0:T(512)(128)(4,1)S(1)} fusion(s32[256]{0:T(256)} %bitcast.5), kind=kLoop, calls=%fused_computation.5 | loop fusion | flops 1536 | bytes 1280 | tf_op jit(solution)/shard_map/jit(_take)/and | solution.py:246
  1.5 0.7 %compare_select_fusion = s32[256,1]{0,1:T(1,128)S(1)} fusion(s32[1,256]{1,0:T(1,128)} %param.8), kind=kLoop, calls=%fused_computation.2 | loop fusion | flops 768 | bytes 2048 | tf_op jit(solution)/shard_map/jit(_take)/jit(_where)/select_n | solution.py:246
  2.2 2.6 %gather_fusion = bf16[256,384]{1,0:T(8,128)(2,1)S(1)} fusion(bf16[1536,384]{1,0:T(8,128)(2,1)} %snap_ref.1, s32[1024]{0:T(1024)S(1)} %pad_clamp_fusion), kind=kCustom, calls=%fused_computation | custom fusion | bytes 394240 | tf_op jit(solution)/shard_map/jit(_take)/gather | solution.py:246
  4.7 0.1 broadcast_select_fusion.out_rows_ref
  4.9 0.0 copy-done
  4.9 0.0 copy-done.1
  4.9 0.0 copy-start.2
  4.9 1.0 %copy-done.2 = bf16[125,1536]{1,0:T(8,128)(2,1)S(1)} copy-done((bf16[125,1536]{1,0:T(8,128)(2,1)S(1)}, bf16[125,1536]{1,0:T(8,128)(2,1)}, u32[]{:S(2)}) %copy-start.2) | copy-done | bytes 384024
  5.9 49.8 %shard_map.55 = f32[3,48,384]{2,1,0:T(8,128)S(1)} custom-call(bf16[1536,384]{1,0:T(8,128)(2,1)S(1)} %copy-done, bf16[256,384]{1,0:T(8,128)(2,1)S(1)} %broadcast_select_fusion.out_rows_ref, s32[125,1536]{1,0:T(8,128)S(1)} %copy-done.1, bf16[125,1536]{1,0:T(8,128)(2,1)S(1)} %copy-done.2, s32[1]{0:T(128)S(6)} %copy.7.counts_ref), custom_call_target="tpu_custom_call" | custom-call | tf_op jit(solution)/shard_map/pallas_call | solution.py:249
  55.7 0.7 %copy.8 = f32[3,48,384]{2,1,0:T(8,128)} copy(f32[3,48,384]{2,1,0:T(8,128)S(1)} %shard_map.55) | data formatting | bytes 442368
  (1 shorter events, 0.0 us)
Async XLA Ops:
  0.0 4.9 %copy-start = (bf16[1536,384]{1,0:T(8,128)(2,1)S(1)}, bf16[1536,384]{1,0:T(8,128)(2,1)}, u32[]{:S(2)}) copy-start(bf16[1536,384]{1,0:T(8,128)(2,1)} %snap_ref.1) | copy-start | bytes 3538948
  0.0 4.9 %copy-start.1 = (s32[125,1536]{1,0:T(8,128)S(1)}, s32[125,1536]{1,0:T(8,128)}, u32[]{:S(2)}) copy-start(s32[125,1536]{1,0:T(8,128)} %cols_ref.1) | copy-start | bytes 2304004
  4.9 1.0 %copy-start.2 = (bf16[125,1536]{1,0:T(8,128)(2,1)S(1)}, bf16[125,1536]{1,0:T(8,128)(2,1)}, u32[]{:S(2)}) copy-start(bf16[125,1536]{1,0:T(8,128)(2,1)} %mass_ref.1) | copy-start | bytes 1152004

commit v3 on v2

v3 whole, which is shorter than its diff:
```python
import functools

import jax
import jax.numpy as jnp
from jax import lax
from jax.experimental import pallas as pl
from jax.experimental.pallas import tpu as pltpu
from jax.sharding import PartitionSpec as P

BAND = 3
LANES = 128
STEP = 16
MESH = pl.DeviceIdType.MESH
NT = (((1,), (1,)), ((), ()))
TN = (((0,), (0,)), ((), ()))


def operator_chunk(cols_ref, mass_ref, op_ref, start, cols_pad, mass_pad, cols_t, mass_t, acc):
    nnz = cols_ref.shape[0]
    tile = cols_t.shape[0]
    tiles = op_ref.shape[1] // LANES
    cols_pad[:nnz, :] = cols_ref[:, pl.ds(start, tile)]
    mass_pad[:nnz, :] = mass_ref[:, pl.ds(start, tile)].astype(jnp.float32)
    cols_t[...] = cols_pad[...].T
    mass_t[...] = mass_pad[...].T
    iota = lax.broadcasted_iota(jnp.int32, (LANES, LANES), 0).astype(jnp.float32).astype(jnp.bfloat16)
    zero = jnp.zeros((STEP, LANES), jnp.bfloat16)
    one = jnp.ones((LANES, LANES), jnp.bfloat16)
    zeros = jnp.zeros((LANES, LANES), jnp.bfloat16)

    def group(g, carry):
        base = pl.multiple_of(g * STEP, STEP)
        c = cols_t[pl.ds(base, STEP), :]
        low = (c & (LANES - 1)).astype(jnp.float32)
        high = (c >> 7).astype(jnp.float32)
        m = mass_t[pl.ds(base, STEP), :]

        def wide(x, i):
            return jnp.broadcast_to(x[i : i + 1], (16, LANES)).astype(jnp.bfloat16)

        def left(i):
            return jnp.where(wide(high, i) == iota[:16], wide(m, i), zero)

        def right(i):
            return jnp.where(jnp.concatenate([wide(low, i)] * (LANES // 16), 0) == iota, one, zeros)

        for i in range(0, STEP, 2):
            out = lax.dot_general(
                jnp.concatenate([left(i), left(i + 1)], 0),
                jnp.concatenate([right(i), right(i + 1)], 0),
                NT,
                preferred_element_type=jnp.float32,
            )
            at = pl.multiple_of(base * 16 + i * 16, 32)
            acc[pl.ds(at, 16), :] = out[:16, :LANES]
            acc[pl.ds(at + 16, 16), :] = out[16:, LANES:]
        return carry

    lax.fori_loop(0, tile // STEP, group, 0)
    for h in range(tiles):
        op_ref[pl.ds(start, tile), h * LANES : (h + 1) * LANES] = acc[pl.ds(h, tile, stride=16), :].astype(op_ref.dtype)


def kernel(
    parts, snaps, snap_ref, send_ref, cols_ref, mass_ref, counts_ref, out_ref,
    outgoing, ext, op, x1, x2, image, gram, mine, theirs, visiting, pair, recv, recv_own,
    cols_pad, mass_pad, cols_t, mass_t, acc,
    halo_send, halo_recv, x_send, x_recv, op_send, op_recv,
    swap_send, swap_recv, term_send, term_recv, own_send, own_recv,
):
    me = lax.axis_index("rows")
    here = lax.axis_index("snap")
    rows_cap, width = snap_ref.shape
    halo = outgoing.shape[0] // 2
    share = out_ref.shape[1]
    half = rows_cap // 2
    tile = LANES
    chunks = half // tile
    groups = parts // 2
    count = counts_ref[0]
    odd = lax.rem(here, 2)
    mate = here + 1 - 2 * odd
    side = lax.rem(me, 2)
    group = lax.div(me, 2)
    partner = me + 1 - 2 * side
    after, before = lax.rem(me + 1, parts), lax.rem(me + parts - 1, parts)

    def remote(src, dst, send, arrive, row, snap):
        return pltpu.make_async_remote_copy(
            src_ref=src, dst_ref=dst, send_sem=send, recv_sem=arrive, device_id=(row, snap), device_id_type=MESH
        )

    def back(k):
        return lax.rem(here + snaps - k, snaps)

    def forward(k):
        return lax.rem(here + k, snaps)

    def member(d):
        return 2 * lax.rem(group + d, groups) + side

    barrier = pltpu.get_barrier_semaphore()

    def greet(row, snap):
        pl.semaphore_signal(barrier, inc=1, device_id=(row, snap), device_id_type=MESH)

    greet(after, here)
    greet(before, here)
    for k in range(1, BAND):
        greet(me, forward(k))
        greet(me, back(k))

    def greet_groups(d, carry):
        for k in range(BAND):
            greet(member(groups - d), back(k))
        return carry

    lax.fori_loop(1, groups, greet_groups, 0)
    pl.semaphore_wait(barrier, 2 + 2 * (BAND - 1) + BAND * (groups - 1))

    first = remote(snap_ref, x1, x_send.at[0], x_recv.at[0], me, back(1))
    second = remote(snap_ref, x2, x_send.at[1], x_recv.at[1], me, back(2))
    relay = remote(x1, x2, x_send.at[2], x_recv.at[1], me, back(1))
    up = remote(
        outgoing.at[pl.ds(halo, halo)], ext.at[pl.ds(rows_cap, halo)], halo_send.at[0], halo_recv.at[0], after, here
    )
    down = remote(
        outgoing.at[pl.ds(0, halo)], ext.at[pl.ds(rows_cap + halo, halo)], halo_send.at[1], halo_recv.at[1], before, here
    )
    first.start()

    own_half = pl.multiple_of(odd * half, tile)
    other_half = pl.multiple_of((1 - odd) * half, tile)
    wanted = jnp.broadcast_to(send_ref[...].astype(jnp.float32), (tile, 2 * halo)).T
    lane = lax.broadcasted_iota(jnp.int32, (2 * halo, tile), 1).astype(jnp.float32)
    picks = op.at[pl.ds(own_half, 2 * halo), pl.ds(0, rows_cap)]
    for t in range(rows_cap // tile):
        picks[:, t * tile : (t + 1) * tile] = jnp.where(wanted == lane + float(t * tile), 1.0, 0.0).astype(op.dtype)
    outgoing[...] = jnp.dot(picks[...], snap_ref[...], preferred_element_type=jnp.float32).astype(outgoing.dtype)
    up.start()
    down.start()

    cols_pad[...] = jnp.zeros_like(cols_pad)
    mass_pad[...] = jnp.zeros_like(mass_pad)
    row = lax.broadcasted_iota(jnp.int32, (tile, width), 0)

    def mask(t, carry):
        at = pl.multiple_of(t * tile, tile)
        block = snap_ref[pl.ds(at, tile), :].astype(jnp.float32)
        ext[pl.ds(at, tile), :] = jnp.where(row + at < count, block, 0.0).astype(ext.dtype)
        return carry

    lax.fori_loop(0, rows_cap // tile, mask, 0)

    def lend(t):
        rows = op.at[pl.ds(pl.multiple_of(own_half + t * tile, tile), tile)]
        return remote(rows, rows, op_send.at[t], op_recv.at[t], me, mate)

    def build(t, carry):
        at = pl.multiple_of(own_half + t * tile, tile)
        operator_chunk(cols_ref, mass_ref, op, at, cols_pad, mass_pad, cols_t, mass_t, acc)
        lend(t).start()
        return carry

    lax.fori_loop(0, chunks - 2, build, 0)

    @pl.when(odd == 1)
    def _():
        second.start()

    lax.fori_loop(chunks - 2, chunks - 1, build, 0)
    first.wait_recv()

    @pl.when(odd == 1)
    def _():
        relay.start()

    lax.fori_loop(chunks - 1, chunks, build, 0)

    up.wait()
    down.wait()

    @pl.when(me == 0)
    def _():
        ext[pl.ds(rows_cap, halo), :] = jnp.zeros((halo, width), ext.dtype)

    @pl.when(me == parts - 1)
    def _():
        ext[pl.ds(rows_cap + halo, halo), :] = jnp.zeros((halo, width), ext.dtype)

    big = 2 * tile
    row_big = lax.broadcasted_iota(jnp.int32, (big, width), 0)

    def multiply(at):
        value = jnp.dot(op[pl.ds(at, big), :], ext[...], preferred_element_type=jnp.float32)
        image[pl.ds(at, big), :] = jnp.where(row_big + at < count, value, 0.0).astype(image.dtype)

    def own(t, carry):
        multiply(pl.multiple_of(own_half + t * big, big))
        return carry

    def lent(t, carry):
        lend(2 * t).wait_recv()
        lend(2 * t + 1).wait_recv()
        multiply(pl.multiple_of(other_half + t * big, big))
        return carry

    lax.fori_loop(0, half // big, own, 0)
    lax.fori_loop(0, half // big, lent, 0)

    def swap(k):
        return remote(theirs.at[k], visiting.at[k], swap_send.at[k], swap_recv.at[k], partner, here)

    def term(k, d):
        to = lax.rem(group + d, groups)
        return remote(pair.at[k, to], recv.at[k, d], term_send.at[k, d], term_recv.at[k, d], 2 * to + side, forward(k))

    def own_share(k):
        return remote(mine.at[k, group], recv_own.at[k], own_send.at[k], own_recv.at[k], me, forward(k))

    def band(k, x_ref):
        gram[...] = lax.dot_general(x_ref[...], image[...], TN, preferred_element_type=jnp.float32)
        for g in range(groups):
            low = gram[2 * g * share : (2 * g + 1) * share, :]
            high = gram[(2 * g + 1) * share : (2 * g + 2) * share, :]
            mine[k, g] = jnp.where(side == 0, low, high)
            theirs[k, g] = jnp.where(side == 0, high, low).astype(theirs.dtype)
        swap(k).start()

    def spread(k):
        swap(k).wait_recv()
        for g in range(groups):
            total = mine[k, g] + visiting[k, g].astype(jnp.float32)
            mine[k, g] = total
            pair[k, g] = total.astype(pair.dtype)

        def start(d, carry):
            term(k, d).start()
            return carry

        lax.fori_loop(1, groups, start, 0)
        if k > 0:
            own_share(k).start()

    def collect(k):
        if k > 0:
            own_share(k).wait_recv()
            total = recv_own[k]
        else:
            total = mine[k, group]

        def add(d, total):
            term(k, d).wait_recv()
            return total + recv[k, d].astype(jnp.float32)

        out_ref[k] = lax.fori_loop(1, groups, add, total)

    band(0, snap_ref)
    band(1, x1)
    spread(0)
    second.wait_recv()
    band(2, x2)
    spread(1)
    spread(2)
    for k in range(BAND):
        collect(k)

    first.wait_send()

    @pl.when(odd == 1)
    def _():
        second.wait_send()
        relay.wait_send()

    def lent_sent(t, carry):
        lend(t).wait_send()
        return carry

    lax.fori_loop(0, chunks, lent_sent, 0)

    def sent(d, carry):
        for k in range(BAND):
            term(k, d).wait_send()
        return carry

    lax.fori_loop(1, groups, sent, 0)
    for k in range(BAND):
        swap(k).wait_send()
        if k > 0:
            own_share(k).wait_send()


def body(snapshots, mass, counts, send_rows, columns):
    parts, snaps = lax.axis_size("rows"), lax.axis_size("snap")
    rows_cap, width = snapshots.shape
    halo2 = send_rows.shape[1]
    share = width // parts
    groups = parts // 2
    wide = rows_cap + halo2
    chunks = rows_cap // 2 // LANES
    bf16, f32 = jnp.bfloat16, jnp.float32
    vmem = pl.BlockSpec(memory_space=pltpu.VMEM)
    dma = pltpu.SemaphoreType.DMA
    return pl.pallas_call(
        functools.partial(kernel, parts, snaps),
        out_shape=jax.ShapeDtypeStruct((BAND, share, width), f32),
        in_specs=[vmem] * 4 + [pl.BlockSpec(memory_space=pltpu.SMEM)],
        out_specs=vmem,
        scratch_shapes=[
            pltpu.VMEM((halo2, width), bf16),
            pltpu.VMEM((wide, width), bf16),
            pltpu.VMEM((rows_cap, wide), bf16),
            pltpu.VMEM((rows_cap, width), bf16),
            pltpu.VMEM((rows_cap, width), bf16),
            pltpu.VMEM((rows_cap, width), bf16),
            pltpu.VMEM((width, width), f32),
            pltpu.VMEM((BAND, groups, share, width), f32),
            pltpu.VMEM((BAND, groups, share, width), bf16),
            pltpu.VMEM((BAND, groups, share, width), bf16),
            pltpu.VMEM((BAND, groups, share, width), bf16),
            pltpu.VMEM((BAND, groups, share, width), bf16),
            pltpu.VMEM((BAND, share, width), f32),
            pltpu.VMEM((LANES, LANES), jnp.int32),
            pltpu.VMEM((LANES, LANES), f32),
            pltpu.VMEM((LANES, LANES), jnp.int32),
            pltpu.VMEM((LANES, LANES), f32),
            pltpu.VMEM((LANES * 16, LANES), f32),
            dma((2,)),
            dma((2,)),
            dma((3,)),
            dma((2,)),
            dma((chunks,)),
            dma((chunks,)),
            dma((BAND,)),
            dma((BAND,)),
            dma((BAND, groups)),
            dma((BAND, groups)),
            dma((BAND,)),
            dma((BAND,)),
        ],
        compiler_params=pltpu.CompilerParams(
            collective_id=0, has_side_effects=True, vmem_limit_bytes=48 * 1024 * 1024
        ),
    )(snapshots, send_rows, columns, mass, counts)


def solution(mesh):
    return jax.shard_map(
        body,
        mesh=mesh,
        in_specs=(P("rows", "snap"), P(None, "rows"), P("rows"), P("rows", None), P(None, "rows")),
        out_specs=P(None, ("snap", "rows"), None),
        check_vma=False,
    )
```

time: 56.6 us -> 51.9 us (0.917)
  Pallas kernels: 49.8 us -> 46.2 us
  other arithmetic: 1.48 us -> 0 us
    pallas_call x1, Pallas kernels: 49.8 us -> 46.2 us  [body(): pl.pallas_call(functools.partial(kernel, parts, snaps), out_shape=jax.Sha...]
    unnamed x7 -> x9, local copies, waits for them, and re-layouts: 1.69 us -> 4.76 us
    gather x1 -> x0, local copies, waits for them, and re-layouts: 2.57 us -> none  [body(): outgoing = jnp.take(snapshots, send_rows[0], axis=0)]
    select_n x2 -> x0, other arithmetic: 0.79 us -> none  [body(): outgoing = jnp.take(snapshots, send_rows[0], axis=0)]
    and x1 -> x0, other arithmetic: 0.69 us -> none  [body(): outgoing = jnp.take(snapshots, send_rows[0], axis=0)]
where the time goes in v3:
time: 51.9 us; the launch traced here: 51.6 us
  Pallas kernels  46.2 us (89%)
  local copies, waits for them, and re-layouts  4.76 us (9%)
  between operations  0.67 us (1%)
    pallas_call x1, Pallas kernels, body(): pl.pallas_call(functools.partial(kernel, parts, snaps), out_shape=jax.Sha...  46.2 us
    unnamed x9, local copies, waits for them, and re-layouts  4.76 us

profile of v3, /device:TPU:0, one launch (start us, length us, event | category | flops | bytes accessed | tf_op | source)
XLA Modules:
  0.0 51.6 jit_solution(11128478275503637056)
XLA Ops:
  0.7 0.0 copy-start
  0.7 1.3 %copy-done = bf16[1536,384]{1,0:T(8,128)(2,1)S(1)} copy-done((bf16[1536,384]{1,0:T(8,128)(2,1)S(1)}, bf16[1536,384]{1,0:T(8,128)(2,1)}, u32[]{:S(2)}) %copy-start) | copy-done | bytes 1179672
  1.9 0.0 copy-start.1
  1.9 1.1 %copy-done.1 = s32[125,1536]{1,0:T(8,128)S(1)} copy-done((s32[125,1536]{1,0:T(8,128)S(1)}, s32[125,1536]{1,0:T(8,128)}, u32[]{:S(2)}) %copy-start.1) | copy-done | bytes 768024
  3.1 0.0 copy-start.2
  3.1 1.0 %copy-done.2 = bf16[125,1536]{1,0:T(8,128)(2,1)S(1)} copy-done((bf16[125,1536]{1,0:T(8,128)(2,1)S(1)}, bf16[125,1536]{1,0:T(8,128)(2,1)}, u32[]{:S(2)}) %copy-start.2) | copy-done | bytes 384024
  4.1 0.0 copy-start.3
  4.1 0.7 %copy-done.3 = s32[1,256]{1,0:T(1,128)S(1)} copy-done((s32[1,256]{1,0:T(1,128)S(1)}, s32[1,256]{1,0:T(1,128)}, u32[]{:S(2)}) %copy-start.3) | copy-done | bytes 1048
  4.7 46.2 %shard_map.55 = f32[3,48,384]{2,1,0:T(8,128)S(1)} custom-call(bf16[1536,384]{1,0:T(8,128)(2,1)S(1)} %copy-done, s32[1,256]{1,0:T(1,128)S(1)} %copy-done.3, s32[125,1536]{1,0:T(8,128)S(1)} %copy-done.1, bf16[125,1536]{1,0:T(8,128)(2,1)S(1)} %copy-done.2, s32[1]{0:T(128)S(6)} %copy.7.counts_ref), custom_call_target="tpu_custom_call" | custom-call | tf_op jit(solution)/shard_map/pallas_call | solution.py:304
  50.9 0.7 %copy.8 = f32[3,48,384]{2,1,0:T(8,128)} copy(f32[3,48,384]{2,1,0:T(8,128)S(1)} %shard_map.55) | data formatting | bytes 442368
Async XLA Ops:
  0.7 1.3 %copy-start = (bf16[1536,384]{1,0:T(8,128)(2,1)S(1)}, bf16[1536,384]{1,0:T(8,128)(2,1)}, u32[]{:S(2)}) copy-start(bf16[1536,384]{1,0:T(8,128)(2,1)} %snap_ref.1) | copy-start | bytes 3538948
  1.9 1.1 %copy-start.1 = (s32[125,1536]{1,0:T(8,128)S(1)}, s32[125,1536]{1,0:T(8,128)}, u32[]{:S(2)}) copy-start(s32[125,1536]{1,0:T(8,128)} %cols_ref.1) | copy-start | bytes 2304004
  3.1 1.0 %copy-start.2 = (bf16[125,1536]{1,0:T(8,128)(2,1)S(1)}, bf16[125,1536]{1,0:T(8,128)(2,1)}, u32[]{:S(2)}) copy-start(bf16[125,1536]{1,0:T(8,128)(2,1)} %mass_ref.1) | copy-start | bytes 1152004
  4.1 0.7 %copy-start.3 = (s32[1,256]{1,0:T(1,128)S(1)}, s32[1,256]{1,0:T(1,128)}, u32[]{:S(2)}) copy-start(s32[1,256]{1,0:T(1,128)} %send_ref.1) | copy-start | bytes 3076

commit v4 on v3

--- a/solution.py
+++ b/solution.py
@@ -62,12 +62,16 @@
 
 
 def kernel(
-    parts, snaps, snap_ref, send_ref, cols_ref, mass_ref, counts_ref, out_ref,
-    outgoing, ext, op, x1, x2, image, gram, mine, theirs, visiting, pair, recv, recv_own,
+    parts, snaps, snap_hbm, send_ref, cols_hbm, mass_ref, counts_ref, out_ref,
+    snap_ref, cols_ref, load_sem, outgoing, ext, op, x1, x2, image, gram, mine, theirs, visiting, pair, recv, recv_own,
     cols_pad, mass_pad, cols_t, mass_t, acc,
     halo_send, halo_recv, x_send, x_recv, op_send, op_recv,
     swap_send, swap_recv, term_send, term_recv, own_send, own_recv,
 ):
+    load_snap = pltpu.make_async_copy(snap_hbm, snap_ref, load_sem.at[0])
+    load_cols = pltpu.make_async_copy(cols_hbm, cols_ref, load_sem.at[1])
+    load_snap.start()
+    load_cols.start()
     me = lax.axis_index("rows")
     here = lax.axis_index("snap")
     rows_cap, width = snap_ref.shape
@@ -127,6 +131,7 @@
     down = remote(
         outgoing.at[pl.ds(0, halo)], ext.at[pl.ds(rows_cap + halo, halo)], halo_send.at[1], halo_recv.at[1], before, here
     )
+    load_snap.wait()
     first.start()
 
     own_half = pl.multiple_of(odd * half, tile)
@@ -140,6 +145,7 @@
     up.start()
     down.start()
 
+    load_cols.wait()
     cols_pad[...] = jnp.zeros_like(cols_pad)
     mass_pad[...] = jnp.zeros_like(mass_pad)
     row = lax.broadcasted_iota(jnp.int32, (tile, width), 0)
@@ -168,14 +174,12 @@
     def _():
         second.start()
 
-    lax.fori_loop(chunks - 2, chunks - 1, build, 0)
+    lax.fori_loop(chunks - 2, chunks, build, 0)
     first.wait_recv()
 
     @pl.when(odd == 1)
     def _():
         relay.start()
-
-    lax.fori_loop(chunks - 1, chunks, build, 0)
 
     up.wait()
     down.wait()
@@ -300,13 +304,17 @@
     chunks = rows_cap // 2 // LANES
     bf16, f32 = jnp.bfloat16, jnp.float32
     vmem = pl.BlockSpec(memory_space=pltpu.VMEM)
+    hbm = pl.BlockSpec(memory_space=pltpu.HBM)
     dma = pltpu.SemaphoreType.DMA
     return pl.pallas_call(
         functools.partial(kernel, parts, snaps),
         out_shape=jax.ShapeDtypeStruct((BAND, share, width), f32),
-        in_specs=[vmem] * 4 + [pl.BlockSpec(memory_space=pltpu.SMEM)],
+        in_specs=[hbm, vmem, hbm, vmem, pl.BlockSpec(memory_space=pltpu.SMEM)],
         out_specs=vmem,
         scratch_shapes=[
+            pltpu.VMEM(snapshots.shape, bf16),
+            pltpu.VMEM(columns.shape, jnp.int32),
+            dma((2,)),
             pltpu.VMEM((halo2, width), bf16),
             pltpu.VMEM((wide, width), bf16),
             pltpu.VMEM((rows_cap, wide), bf16),
@@ -339,7 +347,7 @@
             dma((BAND,)),
         ],
         compiler_params=pltpu.CompilerParams(
-            collective_id=0, has_side_effects=True, vmem_limit_bytes=48 * 1024 * 1024
+            collective_id=0, has_side_effects=True, vmem_limit_bytes=62 * 1024 * 1024
         ),
     )(snapshots, send_rows, columns, mass, counts)
 

time: 51.9 us -> 50.2 us (0.967)
  local copies, waits for them, and re-layouts: 4.76 us -> 1.64 us
  Pallas kernels: 46.2 us -> 47.8 us
    unnamed x9 -> x1, local copies, waits for them, and re-layouts: 4.76 us -> 1.64 us
    pallas_call x1, Pallas kernels: 46.2 us -> 47.8 us  [body(): pl.pallas_call(functools.partial(kernel, parts, snaps), out_shape=jax.Sha...]
where the time goes in v4:
time: 50.2 us; the launch traced here: 50.1 us
  Pallas kernels  47.8 us (95%)
  local copies, waits for them, and re-layouts  1.64 us (3%)
  between operations  0.66 us (1%)
    pallas_call x1, Pallas kernels, body(): pl.pallas_call(functools.partial(kernel, parts, snaps), out_shape=jax.Sha...  47.8 us
    unnamed x1, local copies, waits for them, and re-layouts  1.64 us

profile of v4, /device:TPU:0, one launch (start us, length us, event | category | flops | bytes accessed | tf_op | source)
XLA Modules:
  0.0 50.1 jit_solution(13504306243073319443)
XLA Ops:
  0.7 47.8 %shard_map.55 = f32[3,48,384]{2,1,0:T(8,128)} custom-call(bf16[1536,384]{1,0:T(8,128)(2,1)} %snap_hbm.1, s32[1,256]{1,0:T(1,128)} %send_ref.1, s32[125,1536]{1,0:T(8,128)} %cols_hbm.1, bf16[125,1536]{1,0:T(8,128)(2,1)} %mass_ref.1, s32[1]{0:T(128)S(6)} %copy.7.counts_ref), custom_call_target="tpu_custom_call" | custom-call | tf_op jit(solution)/shard_map/pallas_call | solution.py:309
  48.4 1.6 %copy.8 = f32[3,48,384]{2,1,0:T(8,128)} copy(f32[3,48,384]{2,1,0:T(8,128)} %shard_map.55) | data formatting | bytes 442368
